TPU v7x, 256 devices: a whole 4x4x8 slice. The times are simulated.
256 devices in a mesh: inst: 32 (over y, z_lo, core), tp: 8 (over x, z_hi).
Axes of the slice: x: 4, y: 4, z: 8 (z_hi: 2, z_lo: 4; z = z_hi * 4 + z_lo), core: 2. Of those that a mesh axis runs over, the one named last changes fastest.
Arguments:
- queries: bfloat16 [256, 8192], P('inst', 'tp'), may hold values from -8 to 8
- key_cache: bfloat16 [256, 512, 1024], P('inst', None, 'tp'), may hold values from -6 to 6
- cache_of_values: bfloat16 [256, 512, 1024], P('inst', None, 'tp'), may hold values from -6 to 6
- fresh_key_rows: bfloat16 [256, 1024], P('inst', 'tp'), may hold values from -6 to 6
- fresh_value_rows: bfloat16 [256, 1024], P('inst', 'tp'), may hold values from -6 to 6
- lengths: int32 [32, 8], replicated, may hold values from 1 to 512, 2304 in all within a row
- migrate_ids: int32 [32, 1], replicated, may hold values from 0 to 7, as said below
- partner: int32 [32], replicated, may hold values from 0 to 31, as said below
- migrant_queries: bfloat16 [32, 8192], P('inst', 'tp'), may hold values from -8 to 8
- mover_key_rows: bfloat16 [32, 1024], P('inst', 'tp'), may hold values from -6 to 6
- mover_value_rows: bfloat16 [32, 1024], P('inst', 'tp'), may hold values from -6 to 6
- out_weight: bfloat16 [8192, 4096], P('tp'), may hold values from -0.0625 to 0.0625
Outputs:
- resident_out: bfloat16 [256, 4096], P('inst')
- migrant_out: bfloat16 [32, 4096], P('inst')
Inputs may be any that keep to these rules, and one draw needn't show every extreme that they name: partner[partner[i]] == i and partner[i] != i; some instance a is matched with a + 16. `migrate_ids`: the 1 ids of one instance are distinct.
All inputs are finite; a program needn't handle non-finite values.
Results may differ from a plain program's by a relative error of at most 0.007.
Values may be sent and summed in bfloat16 or wider, within the bound.
A program may use at most 64 MiB of HBM per device.

v0:
```python
import jax
import jax.numpy as jnp
from jax import lax
from jax.sharding import PartitionSpec as P

HEAD_DIMENSION = 128


def attend(query_rows, key_rows, value_rows, new_key, new_value, seq_lengths):
    token_count = query_rows.shape[0]
    kv_heads = key_rows.shape[2] // HEAD_DIMENSION
    group = query_rows.shape[1] // (kv_heads * HEAD_DIMENSION)
    scaling = HEAD_DIMENSION ** (-0.5)
    query_view = query_rows.reshape(token_count, kv_heads, group, HEAD_DIMENSION)
    key_view = key_rows.reshape(token_count, -1, kv_heads, HEAD_DIMENSION)
    value_view = value_rows.reshape(token_count, -1, kv_heads, HEAD_DIMENSION)
    scores = (
        jnp.einsum("rkgd,rlkd->rkgl", query_view, key_view, preferred_element_type=jnp.float32)
        * scaling
    )
    own = (
        jnp.einsum(
            "rkgd,rkd->rkg",
            query_view,
            new_key.reshape(token_count, kv_heads, HEAD_DIMENSION),
            preferred_element_type=jnp.float32,
        )
        * scaling
    )
    positions = jnp.arange(key_view.shape[1], dtype=jnp.int32)
    visible = (positions[None, :] < seq_lengths[:, None])[:, None, None, :]
    scores = jnp.where(visible, scores, jnp.float32(-1e30))
    top = jnp.maximum(jnp.max(scores, axis=-1), own)
    weights = jnp.where(visible, jnp.exp(scores - top[..., None]), jnp.float32(0.0))
    own_weight = jnp.exp(own - top)
    total = jnp.sum(weights, axis=-1) + own_weight
    probs = (weights / total[..., None]).astype(jnp.bfloat16)
    own_prob = (own_weight / total).astype(jnp.bfloat16)
    mixed = jnp.einsum("rkgl,rlkd->rkgd", probs, value_view, preferred_element_type=jnp.float32)
    mixed = mixed + own_prob.astype(jnp.float32)[..., None] * new_value.astype(jnp.float32).reshape(
        token_count, kv_heads, 1, HEAD_DIMENSION
    )
    return mixed.reshape(token_count, -1).astype(jnp.bfloat16)


def on_device(
    queries,
    key_cache,
    cache_of_values,
    fresh_key_rows,
    fresh_value_rows,
    lengths,
    migrate_ids,
    partner,
    migrant_queries,
    mover_key_rows,
    mover_value_rows,
    out_weight,
):
    own_index = lax.axis_index("inst")
    inst_count = lax.axis_size("inst")
    sender = partner[own_index]
    own_ids = migrate_ids[own_index]
    leaving = jnp.stack(
        [jnp.take(key_cache, own_ids, axis=0), jnp.take(cache_of_values, own_ids, axis=0)]
    )
    arriving_lengths = jnp.take(lengths[sender], migrate_ids[sender], axis=0)
    resident_heads = attend(
        queries, key_cache, cache_of_values, fresh_key_rows, fresh_value_rows, lengths[own_index]
    )
    resident_part = jnp.dot(resident_heads, out_weight, preferred_element_type=jnp.float32)
    target_slot = jnp.arange(inst_count, dtype=jnp.int32) == sender
    outgoing = jnp.where(
        target_slot[:, None, None, None, None], leaving[None], jnp.zeros((), jnp.bfloat16)
    )
    incoming = lax.all_to_all(outgoing, "inst", split_axis=0, concat_axis=0, tiled=True)
    arrived = lax.dynamic_index_in_dim(incoming, sender, 0, keepdims=False)
    migrant_heads = attend(
        migrant_queries, arrived[0], arrived[1], mover_key_rows, mover_value_rows, arriving_lengths
    )
    migrant_part = jnp.dot(migrant_heads, out_weight, preferred_element_type=jnp.float32)
    resident_total, migrant_total = lax.psum((resident_part, migrant_part), "tp")
    return (resident_total.astype(jnp.bfloat16), migrant_total.astype(jnp.bfloat16))


def solution(mesh):
    in_specs = (
        P("inst", "tp"),
        P("inst", None, "tp"),
        P("inst", None, "tp"),
        P("inst", "tp"),
        P("inst", "tp"),
        P(),
        P(),
        P(),
        P("inst", "tp"),
        P("inst", "tp"),
        P("inst", "tp"),
        P("tp", None),
    )
    out_specs = (P("inst", None), P("inst", None))
    return jax.shard_map(
        on_device, mesh=mesh, in_specs=in_specs, out_specs=out_specs, check_vma=False
    )
```

profile of v0, /device:TPU:8, one launch (start us, length us, event | category | flops | bytes accessed | tf_op | source)
XLA Modules:
  0.0 272.5 jit_solution(5441160220923101027)
XLA Ops:
  0.6 0.0 copy-start
  0.6 1.2 dynamic_slice.20
  3.2 0.7 iota_compare_fusion.2
  4.5 1.3 constant_dynamic-slice_fusion.1
  7.8 1.0 select_bitcast_fusion
  8.8 3.9 %broadcast_select_fusion = bf16[32,2,1,512,128]{4,3,2,1,0:T(8,128)(2,1)} fusion(pred[32]{0:T(512)(128)(4,1)S(1)} %iota_compare_fusion.2, bf16[2,512,128]{2,1,0:T(8,128)(2,1)S(1)} %maximum_bitcast_fusion), kind=kLoop, calls=%fused_computation | loop fusion | flops 4194304 | bytes 8650784 | tf_op jit(solution)/shard_map/jit(_where)/select_n | solution.py:73
  12.7 0.0 copy-start.1
  12.7 0.0 copy-start.2
  12.7 9.3 %all-to-all-start = ((bf16[32,2,1,512,128]{4,3,2,1,0:T(8,128)(2,1)}), bf16[32,2,1,512,128]{4,3,2,1,0:T(8,128)(2,1)}, u32[]{:S(2)}, u32[]{:S(2)}) async-start(bf16[32,2,1,512,128]{4,3,2,1,0:T(8,128)(2,1)} %broadcast_select_fusion), calls=%async_computation | async-start | bytes 16777216 | tf_op jit(solution)/shard_map/all_to_all | solution.py:76
  24.0 0.2 dynamic-slice_reduce_fusion
  24.2 0.1 iota_compare_fusion
  24.3 0.1 fusion.15
  24.4 0.5 fusion.34
  24.9 0.2 fusion.7
  25.1 0.3 fusion.2
  25.4 4.6 %fusion.12 = f32[8,4096]{1,0:T(8,128)S(1)} fusion(bf16[1024,4096]{1,0:T(8,128)(2,1)} %param.25, bf16[1,8,8,128]{3,2,1,0:T(8,128)(2,1)S(1)} %fusion.2), kind=kOutput, calls=%fused_computation.25 | convolution fusion | flops 67108864 | bytes 8536064 | tf_op jit(solution)/shard_map/dot_general | solution.py:71
  30.0 0.6 dynamic-slice.8
  31.2 174.1 %all-to-all-done = bf16[32,2,1,512,128]{4,3,2,1,0:T(8,128)(2,1)} async-done(((bf16[32,2,1,512,128]{4,3,2,1,0:T(8,128)(2,1)}), bf16[32,2,1,512,128]{4,3,2,1,0:T(8,128)(2,1)}, u32[]{:S(2)}, u32[]{:S(2)}) %all-to-all-start) | async-done | bytes 8388640 | tf_op jit(solution)/shard_map/all_to_all | solution.py:76
  205.3 1.2 fusion.35
  206.5 0.1 fusion.36
  206.6 0.2 fusion.18
  206.8 1.1 fusion.5
  207.9 4.6 %fusion.37 = f32[1,4096]{1,0:T(1,128)S(1)} fusion(bf16[1024,1]{0,1:T(2,128)(2,1)S(1)} %reshape.285, bf16[1024,4096]{1,0:T(8,128)(2,1)} %param.25), kind=kOutput, calls=%fused_computation.64 | convolution fusion | flops 8388608 | bytes 8407040 | tf_op jit(solution)/shard_map/dot_general | solution.py:81
  212.5 60.0 %all-reduce.2 = (bf16[8,4096]{1,0:T(8,128)(2,1)}, bf16[1,4096]{1,0:T(2,128)(2,1)}) all-reduce(f32[8,4096]{1,0:T(8,128)S(1)} %fusion.12, f32[1,4096]{1,0:T(1,128)S(1)} %fusion.37), channel_id=1, replica_groups=mesh['inst'=32,'tp'=8] {'tp'}, use_global_device_ids=true, to_apply=%region_2.3 | all-reduce | flops 36864 | bytes 221184 | tf_op jit(solution)/shard_map/psum | solution.py:82
  (24 shorter events, 0.1 us)
Async XLA Ops:
  0.6 29.9 %copy-start = (bf16[1,1024]{1,0:T(2,128)(2,1)S(1)}, bf16[1,1024]{1,0:T(2,128)(2,1)}, u32[]{:S(2)}) copy-start(bf16[1,1024]{1,0:T(2,128)(2,1)} %param.22) | copy-start | bytes 6148
  12.7 11.3 %copy-start.4 = (s32[32,8]{0,1:T(8,128)S(1)}, s32[32,8]{0,1:T(8,128)}, u32[]{:S(2)}) copy-start(s32[32,8]{0,1:T(8,128)} %param.19) | copy-start | bytes 3076
  12.7 11.5 %copy-start.5 = (bf16[8,128]{1,0:T(8,128)(2,1)S(1)}, bf16[8,128]{1,0:T(8,128)(2,1)}, u32[]{:S(2)}) copy-start(bf16[8,128]{1,0:T(8,128)(2,1)} %param.18) | copy-start | bytes 6148
  12.7 11.6 %copy-start.3 = (bf16[8,1024]{1,0:T(8,128)(2,1)S(1)}, bf16[8,1024]{1,0:T(8,128)(2,1)}, u32[]{:S(2)}) copy-start(bf16[8,1024]{1,0:T(8,128)(2,1)} %param.14) | copy-start | bytes 49156
  12.7 11.6 %copy-start.6 = (bf16[8,128]{1,0:T(8,128)(2,1)S(1)}, bf16[8,128]{1,0:T(8,128)(2,1)}, u32[]{:S(2)}) copy-start(bf16[8,128]{1,0:T(8,128)(2,1)} %param.17) | copy-start | bytes 6148
  12.7 11.7 %copy-start.1 = (bf16[8,512,128]{2,1,0:T(8,128)(2,1)S(1)}, bf16[8,512,128]{2,1,0:T(8,128)(2,1)}, u32[]{:S(2)}) copy-start(bf16[8,512,128]{2,1,0:T(8,128)(2,1)} %param.15) | copy-start | bytes 3145732
  12.7 12.4 %copy-start.2 = (bf16[8,512,128]{2,1,0:T(8,128)(2,1)S(1)}, bf16[8,512,128]{2,1,0:T(8,128)(2,1)}, u32[]{:S(2)}) copy-start(bf16[8,512,128]{2,1,0:T(8,128)(2,1)} %param.16) | copy-start | bytes 3145732
  12.7 192.6 %all-to-all-start = ((bf16[32,2,1,512,128]{4,3,2,1,0:T(8,128)(2,1)}), bf16[32,2,1,512,128]{4,3,2,1,0:T(8,128)(2,1)}, u32[]{:S(2)}, u32[]{:S(2)}) async-start(bf16[32,2,1,512,128]{4,3,2,1,0:T(8,128)(2,1)} %broadcast_select_fusion), calls=%async_computation | async-start | bytes 16777216 | tf_op jit(solution)/shard_map/all_to_all | solution.py:76
  24.9 6.3 %copy-start.7 = (bf16[1,128]{1,0:T(2,128)(2,1)S(1)}, bf16[1,128]{1,0:T(2,128)(2,1)}, u32[]{:S(2)}) copy-start(bf16[1,128]{1,0:T(2,128)(2,1)} %param.24) | copy-start | bytes 772
  24.9 181.6 %copy-start.8 = (bf16[1,128]{1,0:T(2,128)(2,1)S(1)}, bf16[1,128]{1,0:T(2,128)(2,1)}, u32[]{:S(2)}) copy-start(bf16[1,128]{1,0:T(2,128)(2,1)} %param.23) | copy-start | bytes 772
where the time goes:
time: 273 us
  waiting for transfers between devices  174 us (64%)
  blocking collectives  60 us (22%)
  matrix products  12.4 us (5%)
  starting transfers between devices  9.34 us (3%)
  between operations  7.19 us (3%)
  other arithmetic  6.05 us (2%)
  local copies, waits for them, and re-layouts  3.38 us (1%)
    all_to_all x1, waiting for transfers between devices, on_device(): lax.all_to_all(outgoing, 'inst', split_axis=0, concat_axis=0, tiled=True)  174 us
    psum x1, blocking collectives, on_device(): lax.psum((resident_part, migrant_part), 'tp')  60 us
    all_to_all x1, starting transfers between devices, on_device(): lax.all_to_all(outgoing, 'inst', split_axis=0, concat_axis=0, tiled=True)  9.34 us
  transfers between devices with their start and end apart: 1, of which 1 were waited for; matrix products, arithmetic and copies ran while one was open for 2% of the time, Pallas kernels for 0%

commit v1 on v0

v1 whole, which is shorter than its diff:
```python
import functools

import jax
import jax.numpy as jnp
from jax import lax
from jax.experimental import pallas as pl
from jax.experimental.pallas import tpu as pltpu
from jax.sharding import PartitionSpec as P

HEAD = 128
GROUP = 8
PACK = 16
MESH = pl.DeviceIdType.MESH
F32, BF16 = jnp.float32, jnp.bfloat16


def wait_all(ref, sem):
    pltpu.make_async_copy(ref, ref, sem).wait()


def attend(queries, keys, values, own_keys, own_values, sizes):
    slots = keys[0].shape[0]
    rows = len(queries)
    scaling = HEAD**-0.5
    positions = lax.broadcasted_iota(jnp.int32, (GROUP, slots), 1)
    scores = [
        lax.dot_general(q, k, (((1,), (1,)), ((), ())), preferred_element_type=F32) * scaling
        for q, k in zip(queries, keys)
    ]
    own = [
        jnp.sum(q.astype(F32) * k.astype(F32), axis=1, keepdims=True) * scaling
        for q, k in zip(queries, own_keys)
    ]
    visible = [positions < n for n in sizes]
    scores = [jnp.where(m, s, jnp.float32(-1e30)) for m, s in zip(visible, scores)]
    top = [jnp.maximum(jnp.max(s, axis=1, keepdims=True), o) for s, o in zip(scores, own)]
    weights = [jnp.where(visible[j], jnp.exp(scores[j] - top[j]), 0.0) for j in range(rows)]
    own_weight = [jnp.exp(o - t) for o, t in zip(own, top)]
    total = [jnp.sum(w, axis=1, keepdims=True) + o for w, o in zip(weights, own_weight)]
    probs = [(w / t).astype(BF16) for w, t in zip(weights, total)]
    own_prob = [(o / t).astype(BF16).astype(F32) for o, t in zip(own_weight, total)]
    mixed = [jnp.dot(p, v, preferred_element_type=F32) for p, v in zip(probs, values)]
    return [
        (m + o * v.astype(F32)).astype(BF16) for m, o, v in zip(mixed, own_prob, own_values)
    ]


def kernel(
    n_inst, n_tp,
    queries, key_cache, value_cache, fresh_keys, fresh_values, lengths, migrate_ids, partner,
    migrant_queries, mover_keys, mover_values, weight,
    resident_out, migrant_out,
    q_in, k_in, v_in, mq_in, mk_in, mv_in, k_all, v_all, w_all, len_s, ids_s, partner_s,
    heads_f, q_buf, h_buf, rs_send, rs_buf, ag_buf, ar_buf,
    small_sem, k_sem, v_sem, w_sem, send_sem, recv_sem,
):
    me, mt = lax.axis_index("inst"), lax.axis_index("tp")
    rows = q_in.shape[0]
    dout = w_all.shape[1]
    part = dout // n_tp
    chunk = dout // PACK

    def inst_peer(k):
        return {"inst": lax.rem(me + k, n_inst)}

    def tp_peer(k):
        return {"tp": lax.rem(mt + k, n_tp)}

    barrier = pltpu.get_barrier_semaphore()

    def greet_inst(k, carry):
        pl.semaphore_signal(barrier, inc=1, device_id=inst_peer(k), device_id_type=MESH)
        return carry

    def greet_tp(k, carry):
        pl.semaphore_signal(barrier, inc=1, device_id=tp_peer(k), device_id_type=MESH)
        return carry

    lax.fori_loop(1, n_tp, greet_tp, 0)
    lax.fori_loop(1, n_inst, greet_inst, 0)

    small = [
        pltpu.make_async_copy(src, dst, small_sem.at[n])
        for n, (src, dst) in enumerate(
            (
                (migrant_queries, mq_in), (mover_keys, mk_in), (mover_values, mv_in),
                (queries, q_in), (fresh_keys, k_in), (fresh_values, v_in),
                (lengths, len_s), (migrate_ids, ids_s), (partner, partner_s),
            )
        )
    ]
    for c in small:
        c.start()
    k_copy = pltpu.make_async_copy(key_cache, k_all, k_sem)
    v_copy = pltpu.make_async_copy(value_cache, v_all, v_sem)
    w_copy = pltpu.make_async_copy(weight, w_all, w_sem)
    k_copy.start()
    v_copy.start()
    w_copy.start()

    for c in small[:3]:
        c.wait()
    mq = mq_in[...].astype(F32)
    block = jnp.concatenate(
        [mq[:, h * HEAD : (h + 1) * HEAD] for h in range(GROUP)]
        + [mk_in[...].astype(F32), mv_in[...].astype(F32)]
        + [jnp.zeros((PACK - GROUP - 2, HEAD), F32)],
        axis=0,
    )
    q_buf[me] = block.astype(BF16)
    pl.semaphore_wait(barrier, n_inst + n_tp - 2)

    def send_inst(buf, n):
        def body(k, carry):
            pltpu.make_async_remote_copy(
                buf.at[me], buf.at[me], send_sem.at[n], recv_sem.at[n],
                device_id=inst_peer(k), device_id_type=MESH,
            ).start()
            return carry

        lax.fori_loop(1, n_inst, body, 0)

    send_inst(q_buf, 0)

    for c in small[3:]:
        c.wait()
    k_copy.wait()
    v_copy.wait()
    q32 = q_in[...].astype(F32)
    k32, v32 = k_in[...].astype(F32), v_in[...].astype(F32)
    for h in range(GROUP):
        heads_f[:, h, :] = q32[:, h * HEAD : (h + 1) * HEAD]
    resident = attend(
        [heads_f[j].astype(BF16) for j in range(rows)],
        [k_all[j] for j in range(rows)],
        [v_all[j] for j in range(rows)],
        [k32[j : j + 1] for j in range(rows)],
        [v32[j : j + 1] for j in range(rows)],
        [len_s[me, j] for j in range(rows)],
    )
    for j in range(rows):
        heads_f[j] = resident[j].astype(F32)
    lhs = jnp.concatenate([heads_f[:, h, :] for h in range(GROUP)], axis=1).astype(BF16)
    w_copy.wait()

    def project(u):
        columns = pl.ds(pl.multiple_of(u * part, part), part)
        p = jnp.dot(lhs, w_all[:, columns], preferred_element_type=F32)
        return jnp.concatenate([p[:, : part // 2], p[:, part // 2 :]], axis=0).astype(BF16)

    def scatter(k, carry):
        u = lax.rem(mt + k, n_tp)
        rs_send[u] = project(u)
        pltpu.make_async_remote_copy(
            rs_send.at[u], rs_buf.at[mt], send_sem.at[1], recv_sem.at[1],
            device_id={"tp": u}, device_id_type=MESH,
        ).start()
        return carry

    lax.fori_loop(1, n_tp, scatter, 0)
    rs_buf[mt] = project(mt)

    wait_all(q_buf.at[pl.ds(0, n_inst - 1)], recv_sem.at[0])
    wait_all(q_buf.at[pl.ds(0, n_inst - 1)], send_sem.at[0])
    other = partner_s[me]
    row = ids_s[me, 0]
    arrived = q_buf[other].astype(F32)
    (served,) = attend(
        [arrived[:GROUP].astype(BF16)],
        [k_all[row]],
        [v_all[row]],
        [arrived[GROUP : GROUP + 1]],
        [arrived[GROUP + 1 : GROUP + 2]],
        [len_s[me, row]],
    )
    h_buf[me] = jnp.concatenate([served.astype(F32), jnp.zeros((PACK - GROUP, HEAD), F32)], axis=0).astype(BF16)
    send_inst(h_buf, 2)

    wait_all(rs_buf.at[pl.ds(0, n_tp - 1)], recv_sem.at[1])
    wait_all(rs_buf.at[pl.ds(0, n_tp - 1)], send_sem.at[1])
    total = rs_buf[0].astype(F32)
    for u in range(1, n_tp):
        total = total + rs_buf[u].astype(F32)
    ag_buf[mt] = total.astype(BF16)

    def gather(k, carry):
        pltpu.make_async_remote_copy(
            ag_buf.at[mt], ag_buf.at[mt], send_sem.at[3], recv_sem.at[3],
            device_id=tp_peer(k), device_id_type=MESH,
        ).start()
        return carry

    lax.fori_loop(1, n_tp, gather, 0)

    wait_all(h_buf.at[pl.ds(0, n_inst - 1)], recv_sem.at[2])
    wait_all(h_buf.at[pl.ds(0, n_inst - 1)], send_sem.at[2])
    mine = h_buf[other].astype(F32)
    mine = jnp.concatenate([mine[h : h + 1] for h in range(GROUP)], axis=1)
    mine = jnp.broadcast_to(mine, (PACK, GROUP * HEAD)).astype(BF16)
    row_of = lax.broadcasted_iota(jnp.int32, (PACK, chunk), 0)
    packed = jnp.zeros((PACK, chunk), F32)
    for c in range(PACK):
        p = jnp.dot(mine, w_all[:, c * chunk : (c + 1) * chunk], preferred_element_type=F32)
        packed = jnp.where(row_of == c, p, packed)
    ar_buf[mt] = packed.astype(BF16)

    def spread(k, carry):
        pltpu.make_async_remote_copy(
            ar_buf.at[mt], ar_buf.at[mt], send_sem.at[4], recv_sem.at[4],
            device_id=tp_peer(k), device_id_type=MESH,
        ).start()
        return carry

    lax.fori_loop(1, n_tp, spread, 0)

    wait_all(ag_buf.at[pl.ds(0, n_tp - 1)], recv_sem.at[3])
    wait_all(ag_buf.at[pl.ds(0, n_tp - 1)], send_sem.at[3])
    for u in range(n_tp):
        block = ag_buf[u].astype(F32)
        wide = jnp.concatenate([block[:rows], block[rows:]], axis=1)
        resident_out[:, u * part : (u + 1) * part] = wide.astype(BF16)

    wait_all(ar_buf.at[pl.ds(0, n_tp - 1)], recv_sem.at[4])
    wait_all(ar_buf.at[pl.ds(0, n_tp - 1)], send_sem.at[4])
    total = ar_buf[0].astype(F32)
    for u in range(1, n_tp):
        total = total + ar_buf[u].astype(F32)
    migrant_out[...] = jnp.concatenate([total[c : c + 1] for c in range(PACK)], axis=1).astype(BF16)


def on_device(n_inst, n_tp, *args):
    queries, key_cache, weight = args[0], args[1], args[11]
    rows, slots, _ = key_cache.shape
    dout = weight.shape[1]
    part = dout // n_tp
    vmem = pltpu.VMEM
    dma = pltpu.SemaphoreType.DMA
    return pl.pallas_call(
        functools.partial(kernel, n_inst, n_tp),
        out_shape=(
            jax.ShapeDtypeStruct((rows, dout), BF16),
            jax.ShapeDtypeStruct((1, dout), BF16),
        ),
        in_specs=[pl.BlockSpec(memory_space=pl.ANY)] * 12,
        out_specs=[pl.BlockSpec(memory_space=vmem)] * 2,
        scratch_shapes=[
            vmem((rows, GROUP * HEAD), BF16),
            vmem((rows, HEAD), BF16),
            vmem((rows, HEAD), BF16),
            vmem((1, GROUP * HEAD), BF16),
            vmem((1, HEAD), BF16),
            vmem((1, HEAD), BF16),
            vmem((rows, slots, HEAD), BF16),
            vmem((rows, slots, HEAD), BF16),
            vmem(weight.shape, BF16),
            pltpu.SMEM(args[5].shape, jnp.int32),
            pltpu.SMEM(args[6].shape, jnp.int32),
            pltpu.SMEM(args[7].shape, jnp.int32),
            vmem((rows, GROUP, HEAD), F32),
            vmem((n_inst, PACK, HEAD), BF16),
            vmem((n_inst, PACK, HEAD), BF16),
            vmem((n_tp, PACK, part // 2), BF16),
            vmem((n_tp, PACK, part // 2), BF16),
            vmem((n_tp, PACK, part // 2), BF16),
            vmem((n_tp, PACK, dout // PACK), BF16),
            dma((9,)),
            dma,
            dma,
            dma,
            dma((5,)),
            dma((5,)),
        ],
        compiler_params=pltpu.CompilerParams(
            collective_id=0, has_side_effects=True, vmem_limit_bytes=48 * 1024 * 1024
        ),
    )(*args)


def solution(mesh):
    in_specs = (
        P("inst", "tp"),
        P("inst", None, "tp"),
        P("inst", None, "tp"),
        P("inst", "tp"),
        P("inst", "tp"),
        P(),
        P(),
        P(),
        P("inst", "tp"),
        P("inst", "tp"),
        P("inst", "tp"),
        P("tp", None),
    )
    out_specs = (P("inst", None), P("inst", None))
    return jax.shard_map(
        functools.partial(on_device, mesh.shape["inst"], mesh.shape["tp"]),
        mesh=mesh, in_specs=in_specs, out_specs=out_specs, check_vma=False,
    )
```

time: 273 us -> 40.5 us (0.15)
  the two profiles are of different devices: /device:TPU:8 before, /device:TPU:1 now
where the time goes in v1:
time: 40.5 us; the launch traced here: 40.1 us
  Pallas kernels  29.6 us (73%)
  local copies, waits for them, and re-layouts  9.91 us (24%)
  between operations  0.65 us (2%)
    pallas_call x1, Pallas kernels, on_device(): pl.pallas_call(functools.partial(kernel, n_inst, n_tp), out_shape=(jax.Sh...  29.6 us
    unnamed x22, local copies, waits for them, and re-layouts  9.91 us

profile of v1, /device:TPU:1, one launch (start us, length us, event | category | flops | bytes accessed | tf_op | source)
XLA Modules:
  0.0 40.1 jit_solution(8377685774175389097)
XLA Ops:
  0.6 0.8 %copy.14.lengths = s32[32,8]{1,0:T(8,128)S(1)} copy(s32[32,8]{0,1:T(8,128)} %param.17) | data formatting | bytes 2048 | tf_op args[5]
  1.4 0.7 %copy.15.migrate_ids = s32[32,1]{1,0:T(8,128)S(1)} copy(s32[32,1]{0,1:T(1,128)} %param.18) | data formatting | bytes 256 | tf_op args[6]
  2.1 0.0 copy-start
  2.1 1.2 %copy-done = bf16[8,512,128]{2,1,0:T(8,128)(2,1)S(1)} copy-done((bf16[8,512,128]{2,1,0:T(8,128)(2,1)S(1)}, bf16[8,512,128]{2,1,0:T(8,128)(2,1)}, u32[]{:S(2)}) %copy-start) | copy-done | bytes 1048600
  3.4 0.0 copy-start.1
  3.4 1.2 %copy-done.1 = bf16[8,512,128]{2,1,0:T(8,128)(2,1)S(1)} copy-done((bf16[8,512,128]{2,1,0:T(8,128)(2,1)S(1)}, bf16[8,512,128]{2,1,0:T(8,128)(2,1)}, u32[]{:S(2)}) %copy-start.1) | copy-done | bytes 1048600
  4.6 0.0 copy-start.2
  4.6 0.7 %copy-done.2 = bf16[8,1024]{1,0:T(8,128)(2,1)S(1)} copy-done((bf16[8,1024]{1,0:T(8,128)(2,1)S(1)}, bf16[8,1024]{1,0:T(8,128)(2,1)}, u32[]{:S(2)}) %copy-start.2) | copy-done | bytes 16408
  5.3 0.0 copy-start.3
  5.3 0.7 %copy-done.3 = bf16[1,1024]{1,0:T(2,128)(2,1)S(1)} copy-done((bf16[1,1024]{1,0:T(2,128)(2,1)S(1)}, bf16[1,1024]{1,0:T(2,128)(2,1)}, u32[]{:S(2)}) %copy-start.3) | copy-done | bytes 2072
  6.0 0.0 copy-start.4
  6.0 0.7 %copy-done.4 = bf16[8,128]{1,0:T(8,128)(2,1)S(1)} copy-done((bf16[8,128]{1,0:T(8,128)(2,1)S(1)}, bf16[8,128]{1,0:T(8,128)(2,1)}, u32[]{:S(2)}) %copy-start.4) | copy-done | bytes 2072
  6.7 0.0 copy-start.5
  6.7 0.7 %copy-done.5 = bf16[8,128]{1,0:T(8,128)(2,1)S(1)} copy-done((bf16[8,128]{1,0:T(8,128)(2,1)S(1)}, bf16[8,128]{1,0:T(8,128)(2,1)}, u32[]{:S(2)}) %copy-start.5) | copy-done | bytes 2072
  7.3 0.0 copy-start.6
  7.3 0.7 %copy-done.6 = s32[32]{0:T(128)S(1)} copy-done((s32[32]{0:T(128)S(1)}, s32[32]{0:T(128)}, u32[]{:S(2)}) %copy-start.6) | copy-done | bytes 152
  8.0 0.0 copy-start.7
  8.0 0.7 %copy-done.7 = bf16[1,128]{1,0:T(2,128)(2,1)S(1)} copy-done((bf16[1,128]{1,0:T(2,128)(2,1)S(1)}, bf16[1,128]{1,0:T(2,128)(2,1)}, u32[]{:S(2)}) %copy-start.7) | copy-done | bytes 280
  8.7 0.0 copy-start.8
  8.7 0.7 %copy-done.8 = bf16[1,128]{1,0:T(2,128)(2,1)S(1)} copy-done((bf16[1,128]{1,0:T(2,128)(2,1)S(1)}, bf16[1,128]{1,0:T(2,128)(2,1)}, u32[]{:S(2)}) %copy-start.8) | copy-done | bytes 280
  9.3 29.6 %shard_map.131 = (bf16[8,4096]{1,0:T(8,128)(2,1)S(1)}, bf16[1,4096]{1,0:T(2,128)(2,1)S(1)}) custom-call(bf16[8,1024]{1,0:T(8,128)(2,1)S(1)} %copy-done.2, bf16[8,512,128]{2,1,0:T(8,128)(2,1)S(1)} %copy-done, bf16[8,512,128]{2,1,0:T(8,128)(2,1)S(1)} %copy-done.1, bf16[8,128]{1,0:T(8,128)(2,1)S(1)} %copy-done.4, bf16[8,128]{1,0:T(8,128)(2,1)S(1)} %copy-done.5, ...), custom_call_target="tpu_custom_call" | custom-call | tf_op jit(solution)/shard_map/pallas_call | solution.py:238
  38.9 0.6 %copy.18 = bf16[8,4096]{1,0:T(8,128)(2,1)} copy(bf16[8,4096]{1,0:T(8,128)(2,1)S(1)} %get-tuple-element.4) | data formatting | bytes 131072
  39.5 0.6 %copy.19 = bf16[1,4096]{1,0:T(2,128)(2,1)} copy(bf16[1,4096]{1,0:T(2,128)(2,1)S(1)} %get-tuple-element.5) | data formatting | bytes 16384
Async XLA Ops:
  2.1 1.2 %copy-start = (bf16[8,512,128]{2,1,0:T(8,128)(2,1)S(1)}, bf16[8,512,128]{2,1,0:T(8,128)(2,1)}, u32[]{:S(2)}) copy-start(bf16[8,512,128]{2,1,0:T(8,128)(2,1)} %key_cache.1) | copy-start | bytes 3145732
  3.4 1.2 %copy-start.1 = (bf16[8,512,128]{2,1,0:T(8,128)(2,1)S(1)}, bf16[8,512,128]{2,1,0:T(8,128)(2,1)}, u32[]{:S(2)}) copy-start(bf16[8,512,128]{2,1,0:T(8,128)(2,1)} %value_cache.1) | copy-start | bytes 3145732
  4.6 0.7 %copy-start.2 = (bf16[8,1024]{1,0:T(8,128)(2,1)S(1)}, bf16[8,1024]{1,0:T(8,128)(2,1)}, u32[]{:S(2)}) copy-start(bf16[8,1024]{1,0:T(8,128)(2,1)} %queries.1) | copy-start | bytes 49156
  5.3 0.7 %copy-start.3 = (bf16[1,1024]{1,0:T(2,128)(2,1)S(1)}, bf16[1,1024]{1,0:T(2,128)(2,1)}, u32[]{:S(2)}) copy-start(bf16[1,1024]{1,0:T(2,128)(2,1)} %migrant_queries.1) | copy-start | bytes 6148
  6.0 0.7 %copy-start.4 = (bf16[8,128]{1,0:T(8,128)(2,1)S(1)}, bf16[8,128]{1,0:T(8,128)(2,1)}, u32[]{:S(2)}) copy-start(bf16[8,128]{1,0:T(8,128)(2,1)} %fresh_keys.1) | copy-start | bytes 6148
  6.7 0.7 %copy-start.5 = (bf16[8,128]{1,0:T(8,128)(2,1)S(1)}, bf16[8,128]{1,0:T(8,128)(2,1)}, u32[]{:S(2)}) copy-start(bf16[8,128]{1,0:T(8,128)(2,1)} %fresh_values.1) | copy-start | bytes 6148
  7.3 0.7 %copy-start.6 = (s32[32]{0:T(128)S(1)}, s32[32]{0:T(128)}, u32[]{:S(2)}) copy-start(s32[32]{0:T(128)} %partner.1) | copy-start | bytes 388
  8.0 0.7 %copy-start.7 = (bf16[1,128]{1,0:T(2,128)(2,1)S(1)}, bf16[1,128]{1,0:T(2,128)(2,1)}, u32[]{:S(2)}) copy-start(bf16[1,128]{1,0:T(2,128)(2,1)} %mover_keys.1) | copy-start | bytes 772
  8.7 0.7 %copy-start.8 = (bf16[1,128]{1,0:T(2,128)(2,1)S(1)}, bf16[1,128]{1,0:T(2,128)(2,1)}, u32[]{:S(2)}) copy-start(bf16[1,128]{1,0:T(2,128)(2,1)} %mover_values.1) | copy-start | bytes 772

commit v2 on v1

v2 whole, which is shorter than its diff:
```python
import functools

import jax
import jax.numpy as jnp
from jax import lax
from jax.experimental import pallas as pl
from jax.experimental.pallas import tpu as pltpu
from jax.sharding import PartitionSpec as P

HEAD = 128
GROUP = 8
PACK = 16
MESH = pl.DeviceIdType.MESH
F32, BF16 = jnp.float32, jnp.bfloat16


def wait_all(ref, sem):
    pltpu.make_async_copy(ref, ref, sem).wait()


def attend(queries, keys, values, own_keys, own_values, sizes):
    slots = keys[0].shape[0]
    rows = len(queries)
    scaling = HEAD**-0.5
    positions = lax.broadcasted_iota(jnp.int32, (GROUP, slots), 1)
    scores = [
        lax.dot_general(q, k, (((1,), (1,)), ((), ())), preferred_element_type=F32) * scaling
        for q, k in zip(queries, keys)
    ]
    own = [
        jnp.sum(q.astype(F32) * k.astype(F32), axis=1, keepdims=True) * scaling
        for q, k in zip(queries, own_keys)
    ]
    visible = [positions < n for n in sizes]
    scores = [jnp.where(m, s, jnp.float32(-1e30)) for m, s in zip(visible, scores)]
    top = [jnp.maximum(jnp.max(s, axis=1, keepdims=True), o) for s, o in zip(scores, own)]
    weights = [jnp.where(visible[j], jnp.exp(scores[j] - top[j]), 0.0) for j in range(rows)]
    own_weight = [jnp.exp(o - t) for o, t in zip(own, top)]
    total = [jnp.sum(w, axis=1, keepdims=True) + o for w, o in zip(weights, own_weight)]
    probs = [(w / t).astype(BF16) for w, t in zip(weights, total)]
    own_prob = [(o / t).astype(BF16).astype(F32) for o, t in zip(own_weight, total)]
    mixed = [jnp.dot(p, v, preferred_element_type=F32) for p, v in zip(probs, values)]
    return [
        (m + o * v.astype(F32)).astype(BF16) for m, o, v in zip(mixed, own_prob, own_values)
    ]


def kernel(
    n_inst, n_tp,
    queries, key_cache, value_cache, fresh_keys, fresh_values, lengths, migrate_ids, partner,
    migrant_queries, mover_keys, mover_values, weight,
    resident_out, migrant_out,
    q_in, k_in, v_in, mq_in, mk_in, mv_in, k_all, v_all, w_all, len_s, ids_s, partner_s,
    heads_f, q_buf, kv_buf, h_buf, x_send, x_buf, z_buf, g_buf, a_buf, b_buf,
    small_sem, k_sem, v_sem, w_sem, send_sem, recv_sem,
):
    me, mt = lax.axis_index("inst"), lax.axis_index("tp")
    n_x = n_tp // 2
    tx, tz = mt // 2, lax.rem(mt, 2)
    rows = q_in.shape[0]
    dout = w_all.shape[1]
    part = dout // n_x
    chunk = dout // PACK

    def send(src, dst, n, device):
        pltpu.make_async_remote_copy(
            src, dst, send_sem.at[n], recv_sem.at[n], device_id=device, device_id_type=MESH
        ).start()

    barrier = pltpu.get_barrier_semaphore()

    def greet_inst(k, carry):
        device = {"inst": lax.rem(me + k, n_inst)}
        pl.semaphore_signal(barrier, inc=1, device_id=device, device_id_type=MESH)
        return carry

    def greet_tp(k, carry):
        device = {"tp": lax.rem(mt + k, n_tp)}
        pl.semaphore_signal(barrier, inc=1, device_id=device, device_id_type=MESH)
        return carry

    lax.fori_loop(1, n_inst, greet_inst, 0)
    lax.fori_loop(1, n_tp, greet_tp, 0)

    small = [
        pltpu.make_async_copy(src, dst, small_sem.at[n])
        for n, (src, dst) in enumerate(
            (
                (migrant_queries, mq_in), (mover_keys, mk_in), (mover_values, mv_in),
                (queries, q_in), (fresh_keys, k_in), (fresh_values, v_in),
                (lengths, len_s), (migrate_ids, ids_s), (partner, partner_s),
            )
        )
    ]
    for c in small:
        c.start()
    k_copy = pltpu.make_async_copy(key_cache, k_all, k_sem)
    v_copy = pltpu.make_async_copy(value_cache, v_all, v_sem)
    w_copy = pltpu.make_async_copy(weight, w_all, w_sem)
    k_copy.start()
    v_copy.start()
    w_copy.start()

    for c in small[:3]:
        c.wait()
    mq = mq_in[...].astype(F32)
    q_buf[me] = jnp.concatenate(
        [mq[:, h * HEAD : (h + 1) * HEAD] for h in range(GROUP)], axis=0
    ).astype(BF16)
    kv_buf[me] = jnp.concatenate([mk_in[...].astype(F32), mv_in[...].astype(F32)], axis=0)
    pl.semaphore_wait(barrier, n_inst + n_tp - 2)
    order = far_first(n_inst)
    for k in order:
        send(q_buf.at[me], q_buf.at[me], 0, {"inst": me ^ k})
    for k in order:
        send(kv_buf.at[me], kv_buf.at[me], 1, {"inst": me ^ k})

    for c in small[3:]:
        c.wait()
    k_copy.wait()
    v_copy.wait()
    q32 = q_in[...].astype(F32)
    k32, v32 = k_in[...].astype(F32), v_in[...].astype(F32)
    for h in range(GROUP):
        heads_f[:, h, :] = q32[:, h * HEAD : (h + 1) * HEAD]
    resident = attend(
        [heads_f[j].astype(BF16) for j in range(rows)],
        [k_all[j] for j in range(rows)],
        [v_all[j] for j in range(rows)],
        [k32[j : j + 1] for j in range(rows)],
        [v32[j : j + 1] for j in range(rows)],
        [len_s[j, me] for j in range(rows)],
    )
    for j in range(rows):
        heads_f[j] = resident[j].astype(F32)
    lhs = jnp.concatenate([heads_f[:, h, :] for h in range(GROUP)], axis=1).astype(BF16)
    w_copy.wait()

    def project(u):
        columns = pl.ds(pl.multiple_of(u * part, part), part)
        p = jnp.dot(lhs, w_all[:, columns], preferred_element_type=F32)
        return jnp.concatenate([p[:, : part // 2], p[:, part // 2 :]], axis=0).astype(BF16)

    for k in range(1, n_x):
        u = lax.rem(tx + k, n_x)
        x_send[k] = project(u)
        send(x_send.at[k], x_buf.at[tx], 2, {"tp": u * 2 + tz})
    x_buf[tx] = project(tx)

    wait_all(x_buf.at[pl.ds(0, n_x - 1)], recv_sem.at[2])
    total = x_buf[0].astype(F32)
    for u in range(1, n_x):
        total = total + x_buf[u].astype(F32)
    z_buf[0] = total.astype(BF16)
    send(z_buf.at[0], z_buf.at[1], 3, {"tp": mt + 1 - 2 * tz})

    other = partner_s[me]
    row = ids_s[0, me]
    wait_all(q_buf.at[pl.ds(0, n_inst - 1)], recv_sem.at[0])
    wait_all(kv_buf.at[pl.ds(0, n_inst - 1)], recv_sem.at[1])
    arrived = kv_buf[other]
    (served,) = attend(
        [q_buf[other]], [k_all[row]], [v_all[row]], [arrived[:1]], [arrived[1:]], [len_s[row, me]]
    )
    h_buf[me] = served
    for k in order:
        send(h_buf.at[me], h_buf.at[me], 4, {"inst": me ^ k})

    wait_all(z_buf.at[1], recv_sem.at[3])
    g_buf[tx] = (z_buf[0].astype(F32) + z_buf[1].astype(F32)).astype(BF16)
    for k in range(1, n_x):
        send(g_buf.at[tx], g_buf.at[tx], 5, {"tp": lax.rem(tx + k, n_x) * 2 + tz})

    wait_all(h_buf.at[pl.ds(0, n_inst - 1)], recv_sem.at[4])
    mine = h_buf[other].astype(F32)
    mine = jnp.concatenate([mine[h : h + 1] for h in range(GROUP)], axis=1)
    mine = jnp.broadcast_to(mine, (PACK, GROUP * HEAD)).astype(BF16)
    row_of = lax.broadcasted_iota(jnp.int32, (PACK, chunk // 2), 0)
    for n, buf in ((6, a_buf), (7, b_buf)):
        packed = jnp.zeros((PACK, chunk // 2), F32)
        for c in range(PACK // 2):
            first = (n - 6) * (dout // 2) + c * chunk
            p = jnp.dot(mine, w_all[:, first : first + chunk], preferred_element_type=F32)
            packed = jnp.where(row_of == 2 * c, p[:, : chunk // 2], packed)
            packed = jnp.where(row_of == 2 * c + 1, p[:, chunk // 2 :], packed)
        buf[mt] = packed.astype(BF16)
        for z in range(2):
            for k in reversed(range(n_x)):
                device = {"tp": lax.rem(tx + k, n_x) * 2 + z}
                if k == 0:
                    pl.when(tz != z)(lambda: send(buf.at[mt], buf.at[mt], n, device))
                else:
                    send(buf.at[mt], buf.at[mt], n, device)

    wait_all(g_buf.at[pl.ds(0, n_x - 1)], recv_sem.at[5])
    for u in range(n_x):
        block = g_buf[u].astype(F32)
        wide = jnp.concatenate([block[:rows], block[rows:]], axis=1)
        resident_out[:, u * part : (u + 1) * part] = wide.astype(BF16)

    for n, buf in ((6, a_buf), (7, b_buf)):
        wait_all(buf.at[pl.ds(0, n_tp - 1)], recv_sem.at[n])
        total = buf[0].astype(F32)
        for u in range(1, n_tp):
            total = total + buf[u].astype(F32)
        first = (n - 6) * (dout // 2)
        migrant_out[:, first : first + dout // 2] = jnp.concatenate(
            [total[c : c + 1] for c in range(PACK)], axis=1
        ).astype(BF16)

    wait_all(q_buf.at[pl.ds(0, n_inst - 1)], send_sem.at[0])
    wait_all(kv_buf.at[pl.ds(0, n_inst - 1)], send_sem.at[1])
    wait_all(x_buf.at[pl.ds(0, n_x - 1)], send_sem.at[2])
    wait_all(z_buf.at[1], send_sem.at[3])
    wait_all(h_buf.at[pl.ds(0, n_inst - 1)], send_sem.at[4])
    wait_all(g_buf.at[pl.ds(0, n_x - 1)], send_sem.at[5])
    wait_all(a_buf.at[pl.ds(0, n_tp - 1)], send_sem.at[6])
    wait_all(b_buf.at[pl.ds(0, n_tp - 1)], send_sem.at[7])


def far_first(n_inst):
    def hops(k):
        y, z = k // 8, k // 2 % 4
        return min(y, n_inst // 8 - y) + z

    return sorted(range(1, n_inst), key=lambda k: -hops(k))


def hand_over(resident, migrant, resident_out, migrant_out, sem):
    copies = [
        pltpu.make_async_copy(resident, resident_out, sem.at[0]),
        pltpu.make_async_copy(migrant, migrant_out, sem.at[1]),
    ]
    for c in copies:
        c.start()
    for c in copies:
        c.wait()


def on_device(n_inst, n_tp, *args):
    args = (*args[:5], args[5].T, args[6].T, *args[7:])
    key_cache, weight = args[1], args[11]
    rows, slots, _ = key_cache.shape
    dout = weight.shape[1]
    n_x = n_tp // 2
    block = (PACK, dout // n_x // 2)
    vmem = pltpu.VMEM
    dma = pltpu.SemaphoreType.DMA
    out_shape = (
        jax.ShapeDtypeStruct((rows, dout), BF16),
        jax.ShapeDtypeStruct((1, dout), BF16),
    )
    outs = pl.pallas_call(
        functools.partial(kernel, n_inst, n_tp),
        out_shape=out_shape,
        in_specs=[pl.BlockSpec(memory_space=pl.ANY)] * 12,
        out_specs=[pl.BlockSpec(memory_space=vmem)] * 2,
        scratch_shapes=[
            vmem((rows, GROUP * HEAD), BF16),
            vmem((rows, HEAD), BF16),
            vmem((rows, HEAD), BF16),
            vmem((1, GROUP * HEAD), BF16),
            vmem((1, HEAD), BF16),
            vmem((1, HEAD), BF16),
            vmem((rows, slots, HEAD), BF16),
            vmem((rows, slots, HEAD), BF16),
            vmem(weight.shape, BF16),
            pltpu.SMEM(args[5].shape, jnp.int32),
            pltpu.SMEM(args[6].shape, jnp.int32),
            pltpu.SMEM(args[7].shape, jnp.int32),
            vmem((rows, GROUP, HEAD), F32),
            vmem((n_inst, GROUP, HEAD), BF16),
            vmem((n_inst, 2, HEAD), F32),
            vmem((n_inst, GROUP, HEAD), BF16),
            vmem((n_x, *block), BF16),
            vmem((n_x, *block), BF16),
            vmem((2, *block), BF16),
            vmem((n_x, *block), BF16),
            vmem((n_tp, PACK, dout // PACK // 2), BF16),
            vmem((n_tp, PACK, dout // PACK // 2), BF16),
            dma((9,)),
            dma,
            dma,
            dma,
            dma((8,)),
            dma((8,)),
        ],
        compiler_params=pltpu.CompilerParams(
            collective_id=0, has_side_effects=True, vmem_limit_bytes=48 * 1024 * 1024
        ),
    )(*[pltpu.with_memory_space_constraint(a, pltpu.HBM) for a in args])
    return pl.pallas_call(
        hand_over,
        out_shape=out_shape,
        in_specs=[pl.BlockSpec(memory_space=vmem)] * 2,
        out_specs=[pl.BlockSpec(memory_space=pl.ANY)] * 2,
        scratch_shapes=[dma((2,))],
        compiler_params=pltpu.CompilerParams(vmem_limit_bytes=4 * 1024 * 1024),
    )(*outs)


def solution(mesh):
    in_specs = (
        P("inst", "tp"),
        P("inst", None, "tp"),
        P("inst", None, "tp"),
        P("inst", "tp"),
        P("inst", "tp"),
        P(),
        P(),
        P(),
        P("inst", "tp"),
        P("inst", "tp"),
        P("inst", "tp"),
        P("tp", None),
    )
    out_specs = (P("inst", None), P("inst", None))
    return jax.shard_map(
        functools.partial(on_device, mesh.shape["inst"], mesh.shape["tp"]),
        mesh=mesh, in_specs=in_specs, out_specs=out_specs, check_vma=False,
    )
```

time: 40.5 us -> 30.7 us (0.76)
  local copies, waits for them, and re-layouts: 9.91 us -> 0 us
    unnamed x22 -> x0, local copies, waits for them, and re-layouts: 9.91 us -> none
    pallas_call x1 -> x2, Pallas kernels: 29.6 us -> 30 us  [the longest x1 29.3 us: on_device(): pl.pallas_call(functools.partial(kernel, n_inst, n_tp), out_shape=out_sha...]
where the time goes in v2:
time: 30.7 us; the launch traced here: 30.6 us
  Pallas kernels  30 us (98%)
  between operations  0.64 us (2%)
    pallas_call x1, Pallas kernels, on_device(): pl.pallas_call(functools.partial(kernel, n_inst, n_tp), out_shape=out_sha...  29.3 us
    pallas_call x1, Pallas kernels, on_device(): pl.pallas_call(hand_over, out_shape=out_shape, in_specs=[pl.BlockSpec(mem...  0.65 us

profile of v2, /device:TPU:1, one launch (start us, length us, event | category | flops | bytes accessed | tf_op | source)
XLA Modules:
  0.0 30.6 jit_solution(2316679533534778581)
XLA Ops:
  0.6 29.3 %shard_map.131 = (bf16[8,4096]{1,0:T(8,128)(2,1)S(1)}, bf16[1,4096]{1,0:T(2,128)(2,1)S(1)}) custom-call(bf16[8,1024]{1,0:T(8,128)(2,1)} %queries.1, bf16[8,512,128]{2,1,0:T(8,128)(2,1)} %key_cache.1, bf16[8,512,128]{2,1,0:T(8,128)(2,1)} %value_cache.1, bf16[8,128]{1,0:T(8,128)(2,1)} %fresh_keys.1, bf16[8,128]{1,0:T(8,128)(2,1)} %fresh_values.1, ...), custom_call_target="tpu_custom_call" | custom-call | tf_op jit(solution)/shard_map/pallas_call | solution.py:253
  29.9 0.7 %shard_map.132 = (bf16[8,4096]{1,0:T(8,128)(2,1)}, bf16[1,4096]{1,0:T(2,128)(2,1)}) custom-call(bf16[8,4096]{1,0:T(8,128)(2,1)S(1)} %get-tuple-element.4.resident, bf16[1,4096]{1,0:T(2,128)(2,1)S(1)} %get-tuple-element.5.migrant), custom_call_target="tpu_custom_call" | custom-call | tf_op jit(solution)/shard_map/pallas_call | solution.py:292

commit v3 on v2

--- a/solution.py
+++ b/solution.py
@@ -69,18 +69,12 @@
 
     barrier = pltpu.get_barrier_semaphore()
 
-    def greet_inst(k, carry):
-        device = {"inst": lax.rem(me + k, n_inst)}
-        pl.semaphore_signal(barrier, inc=1, device_id=device, device_id_type=MESH)
-        return carry
-
-    def greet_tp(k, carry):
+    for k in (*range(1, n_tp, 2), *range(2, n_tp, 2)):
         device = {"tp": lax.rem(mt + k, n_tp)}
         pl.semaphore_signal(barrier, inc=1, device_id=device, device_id_type=MESH)
-        return carry
-
-    lax.fori_loop(1, n_inst, greet_inst, 0)
-    lax.fori_loop(1, n_tp, greet_tp, 0)
+    order = far_first(n_inst)
+    for k in order:
+        pl.semaphore_signal(barrier, inc=1, device_id={"inst": me ^ k}, device_id_type=MESH)
 
     small = [
         pltpu.make_async_copy(src, dst, small_sem.at[n])
@@ -107,13 +101,11 @@
     q_buf[me] = jnp.concatenate(
         [mq[:, h * HEAD : (h + 1) * HEAD] for h in range(GROUP)], axis=0
     ).astype(BF16)
-    kv_buf[me] = jnp.concatenate([mk_in[...].astype(F32), mv_in[...].astype(F32)], axis=0)
+    kv_buf[me] = jnp.concatenate([mk_in[...].astype(F32), mv_in[...].astype(F32)], axis=0).astype(BF16)
     pl.semaphore_wait(barrier, n_inst + n_tp - 2)
-    order = far_first(n_inst)
-    for k in order:
-        send(q_buf.at[me], q_buf.at[me], 0, {"inst": me ^ k})
     for k in order:
         send(kv_buf.at[me], kv_buf.at[me], 1, {"inst": me ^ k})
+        send(q_buf.at[me], q_buf.at[me], 0, {"inst": me ^ k})
 
     for c in small[3:]:
         c.wait()
@@ -147,29 +139,24 @@
         send(x_send.at[k], x_buf.at[tx], 2, {"tp": u * 2 + tz})
     x_buf[tx] = project(tx)
 
+    other = partner_s[me]
+    row = ids_s[0, me]
+    wait_all(q_buf.at[pl.ds(0, n_inst - 1)], recv_sem.at[0])
+    wait_all(kv_buf.at[pl.ds(0, n_inst - 1)], recv_sem.at[1])
+    arrived = kv_buf[other].astype(F32)
+    (served,) = attend(
+        [q_buf[other]], [k_all[row]], [v_all[row]], [arrived[:1]], [arrived[1:]], [len_s[row, me]]
+    )
+    h_buf[me] = served
+    for k in order:
+        send(h_buf.at[me], h_buf.at[me], 4, {"inst": me ^ k})
+
     wait_all(x_buf.at[pl.ds(0, n_x - 1)], recv_sem.at[2])
     total = x_buf[0].astype(F32)
     for u in range(1, n_x):
         total = total + x_buf[u].astype(F32)
     z_buf[0] = total.astype(BF16)
     send(z_buf.at[0], z_buf.at[1], 3, {"tp": mt + 1 - 2 * tz})
-
-    other = partner_s[me]
-    row = ids_s[0, me]
-    wait_all(q_buf.at[pl.ds(0, n_inst - 1)], recv_sem.at[0])
-    wait_all(kv_buf.at[pl.ds(0, n_inst - 1)], recv_sem.at[1])
-    arrived = kv_buf[other]
-    (served,) = attend(
-        [q_buf[other]], [k_all[row]], [v_all[row]], [arrived[:1]], [arrived[1:]], [len_s[row, me]]
-    )
-    h_buf[me] = served
-    for k in order:
-        send(h_buf.at[me], h_buf.at[me], 4, {"inst": me ^ k})
-
-    wait_all(z_buf.at[1], recv_sem.at[3])
-    g_buf[tx] = (z_buf[0].astype(F32) + z_buf[1].astype(F32)).astype(BF16)
-    for k in range(1, n_x):
-        send(g_buf.at[tx], g_buf.at[tx], 5, {"tp": lax.rem(tx + k, n_x) * 2 + tz})
 
     wait_all(h_buf.at[pl.ds(0, n_inst - 1)], recv_sem.at[4])
     mine = h_buf[other].astype(F32)
@@ -192,6 +179,11 @@
                 else:
                     send(buf.at[mt], buf.at[mt], n, device)
 
+    wait_all(z_buf.at[1], recv_sem.at[3])
+    g_buf[tx] = (z_buf[0].astype(F32) + z_buf[1].astype(F32)).astype(BF16)
+    for k in range(1, n_x):
+        send(g_buf.at[tx], g_buf.at[tx], 5, {"tp": lax.rem(tx + k, n_x) * 2 + tz})
+
     wait_all(g_buf.at[pl.ds(0, n_x - 1)], recv_sem.at[5])
     for u in range(n_x):
         block = g_buf[u].astype(F32)
@@ -270,7 +262,7 @@
             pltpu.SMEM(args[7].shape, jnp.int32),
             vmem((rows, GROUP, HEAD), F32),
             vmem((n_inst, GROUP, HEAD), BF16),
-            vmem((n_inst, 2, HEAD), F32),
+            vmem((n_inst, 2, HEAD), BF16),
             vmem((n_inst, GROUP, HEAD), BF16),
             vmem((n_x, *block), BF16),
             vmem((n_x, *block), BF16),

time: 30.7 us -> 29.5 us (0.961)
  Pallas kernels: 30 us -> 28.8 us
    pallas_call x1, Pallas kernels: 29.3 us -> 28.1 us  [on_device(): pl.pallas_call(functools.partial(kernel, n_inst, n_tp), out_shape=out_sha...]
where the time goes in v3:
time: 29.5 us; the launch traced here: 29.4 us
  Pallas kernels  28.8 us (98%)
  between operations  0.64 us (2%)
    pallas_call x1, Pallas kernels, on_device(): pl.pallas_call(functools.partial(kernel, n_inst, n_tp), out_shape=out_sha...  28.1 us
    pallas_call x1, Pallas kernels, on_device(): pl.pallas_call(hand_over, out_shape=out_shape, in_specs=[pl.BlockSpec(mem...  0.65 us

profile of v3, /device:TPU:1, one launch (start us, length us, event | category | flops | bytes accessed | tf_op | source)
XLA Modules:
  0.0 29.4 jit_solution(365400457738311005)
XLA Ops:
  0.6 28.1 %shard_map.131 = (bf16[8,4096]{1,0:T(8,128)(2,1)S(1)}, bf16[1,4096]{1,0:T(2,128)(2,1)S(1)}) custom-call(bf16[8,1024]{1,0:T(8,128)(2,1)} %queries.1, bf16[8,512,128]{2,1,0:T(8,128)(2,1)} %key_cache.1, bf16[8,512,128]{2,1,0:T(8,128)(2,1)} %value_cache.1, bf16[8,128]{1,0:T(8,128)(2,1)} %fresh_keys.1, bf16[8,128]{1,0:T(8,128)(2,1)} %fresh_values.1, ...), custom_call_target="tpu_custom_call" | custom-call | tf_op jit(solution)/shard_map/pallas_call | solution.py:245
  28.8 0.7 %shard_map.132 = (bf16[8,4096]{1,0:T(8,128)(2,1)}, bf16[1,4096]{1,0:T(2,128)(2,1)}) custom-call(bf16[8,4096]{1,0:T(8,128)(2,1)S(1)} %get-tuple-element.4.resident, bf16[1,4096]{1,0:T(2,128)(2,1)S(1)} %get-tuple-element.5.migrant), custom_call_target="tpu_custom_call" | custom-call | tf_op jit(solution)/shard_map/pallas_call | solution.py:284

commit v4 on v3

--- a/solution.py
+++ b/solution.py
@@ -69,9 +69,28 @@
 
     barrier = pltpu.get_barrier_semaphore()
 
+    def served_by(inst, z):
+        first = inst ^ (6 * z)
+        return first, first ^ 2
+
+    def greet(inst, tp):
+        device = {"inst": inst, "tp": tp}
+        pl.semaphore_signal(barrier, inc=1, device_id=device, device_id_type=MESH)
+
     for k in (*range(1, n_tp, 2), *range(2, n_tp, 2)):
-        device = {"tp": lax.rem(mt + k, n_tp)}
-        pl.semaphore_signal(barrier, inc=1, device_id=device, device_id_type=MESH)
+        tp = lax.rem(mt + k, n_tp)
+        for inst in served_by(me, lax.rem(tp, 2)):
+            greet(inst, tp)
+
+    @pl.when(tz == 0)
+    def _():
+        greet(me, mt + 1)
+
+    @pl.when(tz == 1)
+    def _():
+        for k in range(1, n_x):
+            greet(me, lax.rem(tx + k, n_x) * 2 + 1)
+
     order = far_first(n_inst)
     for k in order:
         pl.semaphore_signal(barrier, inc=1, device_id={"inst": me ^ k}, device_id_type=MESH)
@@ -102,7 +121,7 @@
         [mq[:, h * HEAD : (h + 1) * HEAD] for h in range(GROUP)], axis=0
     ).astype(BF16)
     kv_buf[me] = jnp.concatenate([mk_in[...].astype(F32), mv_in[...].astype(F32)], axis=0).astype(BF16)
-    pl.semaphore_wait(barrier, n_inst + n_tp - 2)
+    pl.semaphore_wait(barrier, n_inst - 1 + 2 * (n_tp - 1) + n_x * tz)
     for k in order:
         send(kv_buf.at[me], kv_buf.at[me], 1, {"inst": me ^ k})
         send(q_buf.at[me], q_buf.at[me], 0, {"inst": me ^ k})
@@ -159,25 +178,38 @@
     send(z_buf.at[0], z_buf.at[1], 3, {"tp": mt + 1 - 2 * tz})
 
     wait_all(h_buf.at[pl.ds(0, n_inst - 1)], recv_sem.at[4])
-    mine = h_buf[other].astype(F32)
-    mine = jnp.concatenate([mine[h : h + 1] for h in range(GROUP)], axis=1)
-    mine = jnp.broadcast_to(mine, (PACK, GROUP * HEAD)).astype(BF16)
-    row_of = lax.broadcasted_iota(jnp.int32, (PACK, chunk // 2), 0)
-    for n, buf in ((6, a_buf), (7, b_buf)):
-        packed = jnp.zeros((PACK, chunk // 2), F32)
-        for c in range(PACK // 2):
-            first = (n - 6) * (dout // 2) + c * chunk
-            p = jnp.dot(mine, w_all[:, first : first + chunk], preferred_element_type=F32)
-            packed = jnp.where(row_of == 2 * c, p[:, : chunk // 2], packed)
-            packed = jnp.where(row_of == 2 * c + 1, p[:, chunk // 2 :], packed)
-        buf[mt] = packed.astype(BF16)
-        for z in range(2):
-            for k in reversed(range(n_x)):
-                device = {"tp": lax.rem(tx + k, n_x) * 2 + z}
-                if k == 0:
-                    pl.when(tz != z)(lambda: send(buf.at[mt], buf.at[mt], n, device))
+    half_of = lax.rem(me // 2, 2)
+    pair = served_by(me, tz)
+    heads = [h_buf[partner_s[inst]].astype(F32) for inst in pair]
+    heads = [jnp.concatenate([m[h : h + 1] for h in range(GROUP)], axis=1) for m in heads]
+    heads = jnp.concatenate(
+        [jnp.broadcast_to(m, (PACK // 2, GROUP * HEAD)) for m in heads], axis=0
+    ).astype(BF16)
+    row_of = lax.rem(lax.broadcasted_iota(jnp.int32, (PACK, chunk), 0), PACK // 2)
+    packed = jnp.zeros((PACK, chunk), F32)
+    for c in range(PACK // 2):
+        columns = pl.ds(pl.multiple_of(half_of * (dout // 2) + c * chunk, chunk), chunk)
+        p = jnp.dot(heads, w_all[:, columns], preferred_element_type=F32)
+        packed = jnp.where(row_of == c, p, packed)
+    slot = half_of * n_tp + mt
+    for n in range(2):
+        b_buf[n] = packed[n * PACK // 2 : (n + 1) * PACK // 2].astype(BF16)
+
+    @pl.when(tz == 0)
+    def _():
+        a_buf[slot] = b_buf[0]
+
+    for z in range(2):
+        for k in reversed(range(n_x)):
+            tp = lax.rem(tx + k, n_x) * 2 + z
+            for n in range(2):
+                give = functools.partial(
+                    send, b_buf.at[n], a_buf.at[slot], 6, {"inst": pair[n], "tp": tp}
+                )
+                if (z, k, n) == (0, 0, 0):
+                    pl.when(tz == 1)(give)
                 else:
-                    send(buf.at[mt], buf.at[mt], n, device)
+                    give()
 
     wait_all(z_buf.at[1], recv_sem.at[3])
     g_buf[tx] = (z_buf[0].astype(F32) + z_buf[1].astype(F32)).astype(BF16)
@@ -190,14 +222,18 @@
         wide = jnp.concatenate([block[:rows], block[rows:]], axis=1)
         resident_out[:, u * part : (u + 1) * part] = wide.astype(BF16)
 
-    for n, buf in ((6, a_buf), (7, b_buf)):
-        wait_all(buf.at[pl.ds(0, n_tp - 1)], recv_sem.at[n])
-        total = buf[0].astype(F32)
+    def wait_sums(sem):
+        pl.when(tz == 0)(lambda: wait_all(a_buf.at[pl.ds(0, 2 * n_tp - 1)], sem))
+        pl.when(tz == 1)(lambda: wait_all(a_buf, sem))
+
+    wait_sums(recv_sem.at[6])
+    for half in range(2):
+        total = a_buf[half * n_tp].astype(F32)
         for u in range(1, n_tp):
-            total = total + buf[u].astype(F32)
-        first = (n - 6) * (dout // 2)
+            total = total + a_buf[half * n_tp + u].astype(F32)
+        first = half * (dout // 2)
         migrant_out[:, first : first + dout // 2] = jnp.concatenate(
-            [total[c : c + 1] for c in range(PACK)], axis=1
+            [total[c : c + 1] for c in range(PACK // 2)], axis=1
         ).astype(BF16)
 
     wait_all(q_buf.at[pl.ds(0, n_inst - 1)], send_sem.at[0])
@@ -206,8 +242,7 @@
     wait_all(z_buf.at[1], send_sem.at[3])
     wait_all(h_buf.at[pl.ds(0, n_inst - 1)], send_sem.at[4])
     wait_all(g_buf.at[pl.ds(0, n_x - 1)], send_sem.at[5])
-    wait_all(a_buf.at[pl.ds(0, n_tp - 1)], send_sem.at[6])
-    wait_all(b_buf.at[pl.ds(0, n_tp - 1)], send_sem.at[7])
+    wait_sums(send_sem.at[6])
 
 
 def far_first(n_inst):
@@ -268,14 +303,14 @@
             vmem((n_x, *block), BF16),
             vmem((2, *block), BF16),
             vmem((n_x, *block), BF16),
-            vmem((n_tp, PACK, dout // PACK // 2), BF16),
-            vmem((n_tp, PACK, dout // PACK // 2), BF16),
+            vmem((2 * n_tp, PACK // 2, dout // PACK), BF16),
+            vmem((2, PACK // 2, dout // PACK), BF16),
             dma((9,)),
             dma,
             dma,
             dma,
-            dma((8,)),
-            dma((8,)),
+            dma((7,)),
+            dma((7,)),
         ],
         compiler_params=pltpu.CompilerParams(
             collective_id=0, has_side_effects=True, vmem_limit_bytes=48 * 1024 * 1024

time: 29.5 us -> 28.1 us (0.953)
  Pallas kernels: 28.8 us -> 27.3 us
    pallas_call x1, Pallas kernels: 28.1 us -> 26.7 us  [on_device(): pl.pallas_call(functools.partial(kernel, n_inst, n_tp), out_shape=out_sha...]
where the time goes in v4:
time: 28.1 us; the launch traced here: 28 us
  Pallas kernels  27.3 us (97%)
  between operations  0.64 us (2%)
    pallas_call x1, Pallas kernels, on_device(): pl.pallas_call(functools.partial(kernel, n_inst, n_tp), out_shape=out_sha...  26.7 us
    pallas_call x1, Pallas kernels, on_device(): pl.pallas_call(hand_over, out_shape=out_shape, in_specs=[pl.BlockSpec(mem...  0.65 us

profile of v4, /device:TPU:1, one launch (start us, length us, event | category | flops | bytes accessed | tf_op | source)
XLA Modules:
  0.0 28.0 jit_solution(12998507735382171901)
XLA Ops:
  0.6 26.7 %shard_map.131 = (bf16[8,4096]{1,0:T(8,128)(2,1)S(1)}, bf16[1,4096]{1,0:T(2,128)(2,1)S(1)}) custom-call(bf16[8,1024]{1,0:T(8,128)(2,1)} %queries.1, bf16[8,512,128]{2,1,0:T(8,128)(2,1)} %key_cache.1, bf16[8,512,128]{2,1,0:T(8,128)(2,1)} %value_cache.1, bf16[8,128]{1,0:T(8,128)(2,1)} %fresh_keys.1, bf16[8,128]{1,0:T(8,128)(2,1)} %fresh_values.1, ...), custom_call_target="tpu_custom_call" | custom-call | tf_op jit(solution)/shard_map/pallas_call | solution.py:280
  27.3 0.7 %shard_map.132 = (bf16[8,4096]{1,0:T(8,128)(2,1)}, bf16[1,4096]{1,0:T(2,128)(2,1)}) custom-call(bf16[8,4096]{1,0:T(8,128)(2,1)S(1)} %get-tuple-element.4.resident, bf16[1,4096]{1,0:T(2,128)(2,1)S(1)} %get-tuple-element.5.migrant), custom_call_target="tpu_custom_call" | custom-call | tf_op jit(solution)/shard_map/pallas_call | solution.py:319

commit v5 on v4

--- a/solution.py
+++ b/solution.py
@@ -77,6 +77,9 @@
         device = {"inst": inst, "tp": tp}
         pl.semaphore_signal(barrier, inc=1, device_id=device, device_id_type=MESH)
 
+    order = far_first(n_inst)
+    for k in order:
+        greet(me ^ k, mt)
     for k in (*range(1, n_tp, 2), *range(2, n_tp, 2)):
         tp = lax.rem(mt + k, n_tp)
         for inst in served_by(me, lax.rem(tp, 2)):
@@ -90,10 +93,6 @@
     def _():
         for k in range(1, n_x):
             greet(me, lax.rem(tx + k, n_x) * 2 + 1)
-
-    order = far_first(n_inst)
-    for k in order:
-        pl.semaphore_signal(barrier, inc=1, device_id={"inst": me ^ k}, device_id_type=MESH)
 
     small = [
         pltpu.make_async_copy(src, dst, small_sem.at[n])

time: 28.1 us -> 27.9 us (level)
  no operation moved by 1% of the time
where the time goes in v5:
time: 27.9 us; the launch traced here: 27.8 us
  Pallas kernels  27.1 us (97%)
  between operations  0.64 us (2%)
    pallas_call x1, Pallas kernels, on_device(): pl.pallas_call(functools.partial(kernel, n_inst, n_tp), out_shape=out_sha...  26.5 us
    pallas_call x1, Pallas kernels, on_device(): pl.pallas_call(hand_over, out_shape=out_shape, in_specs=[pl.BlockSpec(mem...  0.65 us

profile of v5, /device:TPU:1, one launch (start us, length us, event | category | flops | bytes accessed | tf_op | source)
XLA Modules:
  0.0 27.8 jit_solution(15999221789479316894)
XLA Ops:
  0.6 26.5 %shard_map.131 = (bf16[8,4096]{1,0:T(8,128)(2,1)S(1)}, bf16[1,4096]{1,0:T(2,128)(2,1)S(1)}) custom-call(bf16[8,1024]{1,0:T(8,128)(2,1)} %queries.1, bf16[8,512,128]{2,1,0:T(8,128)(2,1)} %key_cache.1, bf16[8,512,128]{2,1,0:T(8,128)(2,1)} %value_cache.1, bf16[8,128]{1,0:T(8,128)(2,1)} %fresh_keys.1, bf16[8,128]{1,0:T(8,128)(2,1)} %fresh_values.1, ...), custom_call_target="tpu_custom_call" | custom-call | tf_op jit(solution)/shard_map/pallas_call | solution.py:279
  27.1 0.7 %shard_map.132 = (bf16[8,4096]{1,0:T(8,128)(2,1)}, bf16[1,4096]{1,0:T(2,128)(2,1)}) custom-call(bf16[8,4096]{1,0:T(8,128)(2,1)S(1)} %get-tuple-element.4.resident, bf16[1,4096]{1,0:T(2,128)(2,1)S(1)} %get-tuple-element.5.migrant), custom_call_target="tpu_custom_call" | custom-call | tf_op jit(solution)/shard_map/pallas_call | solution.py:318

commit v6 on v5

--- a/solution.py
+++ b/solution.py
@@ -166,8 +166,8 @@
         [q_buf[other]], [k_all[row]], [v_all[row]], [arrived[:1]], [arrived[1:]], [len_s[row, me]]
     )
     h_buf[me] = served
-    for k in order:
-        send(h_buf.at[me], h_buf.at[me], 4, {"inst": me ^ k})
+    for u in first_served(n_inst):
+        pl.when(me != u)(lambda: send(h_buf.at[me], h_buf.at[me], 4, {"inst": u}))
 
     wait_all(x_buf.at[pl.ds(0, n_x - 1)], recv_sem.at[2])
     total = x_buf[0].astype(F32)
@@ -199,14 +199,14 @@
         a_buf[slot] = b_buf[0]
 
     for z in range(2):
-        for k in reversed(range(n_x)):
-            tp = lax.rem(tx + k, n_x) * 2 + z
+        for u in range(n_x):
+            tp = u * 2 + z
             for n in range(2):
                 give = functools.partial(
                     send, b_buf.at[n], a_buf.at[slot], 6, {"inst": pair[n], "tp": tp}
                 )
-                if (z, k, n) == (0, 0, 0):
-                    pl.when(tz == 1)(give)
+                if z == 0 and n == 0:
+                    pl.when(mt != tp)(give)
                 else:
                     give()
 
@@ -224,16 +224,6 @@
     def wait_sums(sem):
         pl.when(tz == 0)(lambda: wait_all(a_buf.at[pl.ds(0, 2 * n_tp - 1)], sem))
         pl.when(tz == 1)(lambda: wait_all(a_buf, sem))
-
-    wait_sums(recv_sem.at[6])
-    for half in range(2):
-        total = a_buf[half * n_tp].astype(F32)
-        for u in range(1, n_tp):
-            total = total + a_buf[half * n_tp + u].astype(F32)
-        first = half * (dout // 2)
-        migrant_out[:, first : first + dout // 2] = jnp.concatenate(
-            [total[c : c + 1] for c in range(PACK // 2)], axis=1
-        ).astype(BF16)
 
     wait_all(q_buf.at[pl.ds(0, n_inst - 1)], send_sem.at[0])
     wait_all(kv_buf.at[pl.ds(0, n_inst - 1)], send_sem.at[1])
@@ -241,7 +231,21 @@
     wait_all(z_buf.at[1], send_sem.at[3])
     wait_all(h_buf.at[pl.ds(0, n_inst - 1)], send_sem.at[4])
     wait_all(g_buf.at[pl.ds(0, n_x - 1)], send_sem.at[5])
+    wait_sums(recv_sem.at[6])
+    for half in range(2):
+        terms = [a_buf[half * n_tp + u].astype(F32) for u in range(n_tp)]
+        while len(terms) > 1:
+            terms = [a + b for a, b in zip(terms[::2], terms[1::2])]
+        for c in range(PACK // 2):
+            first = half * (dout // 2) + c * chunk
+            migrant_out[:, first : first + chunk] = terms[0][c : c + 1].astype(BF16)
+
     wait_sums(send_sem.at[6])
+
+
+def first_served(n_inst):
+    head = [7, 5, 1, 3]
+    return head + [u for u in range(n_inst) if u not in head]
 
 
 def far_first(n_inst):

time: 27.9 us -> 27.1 us (0.971)
  Pallas kernels: 27.1 us -> 26.4 us
    pallas_call x1, Pallas kernels: 26.5 us -> 25.7 us  [on_device(): pl.pallas_call(functools.partial(kernel, n_inst, n_tp), out_shape=out_sha...]
where the time goes in v6:
time: 27.1 us; the launch traced here: 27 us
  Pallas kernels  26.4 us (97%)
  between operations  0.64 us (2%)
    pallas_call x1, Pallas kernels, on_device(): pl.pallas_call(functools.partial(kernel, n_inst, n_tp), out_shape=out_sha...  25.7 us
    pallas_call x1, Pallas kernels, on_device(): pl.pallas_call(hand_over, out_shape=out_shape, in_specs=[pl.BlockSpec(mem...  0.65 us

profile of v6, /device:TPU:1, one launch (start us, length us, event | category | flops | bytes accessed | tf_op | source)
XLA Modules:
  0.0 27.0 jit_solution(5217118690491932770)
XLA Ops:
  0.6 25.7 %shard_map.131 = (bf16[8,4096]{1,0:T(8,128)(2,1)S(1)}, bf16[1,4096]{1,0:T(2,128)(2,1)S(1)}) custom-call(bf16[8,1024]{1,0:T(8,128)(2,1)} %queries.1, bf16[8,512,128]{2,1,0:T(8,128)(2,1)} %key_cache.1, bf16[8,512,128]{2,1,0:T(8,128)(2,1)} %value_cache.1, bf16[8,128]{1,0:T(8,128)(2,1)} %fresh_keys.1, bf16[8,128]{1,0:T(8,128)(2,1)} %fresh_values.1, ...), custom_call_target="tpu_custom_call" | custom-call | tf_op jit(solution)/shard_map/pallas_call | solution.py:283
  26.4 0.7 %shard_map.132 = (bf16[8,4096]{1,0:T(8,128)(2,1)}, bf16[1,4096]{1,0:T(2,128)(2,1)}) custom-call(bf16[8,4096]{1,0:T(8,128)(2,1)S(1)} %get-tuple-element.4.resident, bf16[1,4096]{1,0:T(2,128)(2,1)S(1)} %get-tuple-element.5.migrant), custom_call_target="tpu_custom_call" | custom-call | tf_op jit(solution)/shard_map/pallas_call | solution.py:322

commit v7 on v6

--- a/solution.py
+++ b/solution.py
@@ -34,11 +34,12 @@
     visible = [positions < n for n in sizes]
     scores = [jnp.where(m, s, jnp.float32(-1e30)) for m, s in zip(visible, scores)]
     top = [jnp.maximum(jnp.max(s, axis=1, keepdims=True), o) for s, o in zip(scores, own)]
-    weights = [jnp.where(visible[j], jnp.exp(scores[j] - top[j]), 0.0) for j in range(rows)]
+    weights = [jnp.exp(scores[j] - top[j]) for j in range(rows)]
     own_weight = [jnp.exp(o - t) for o, t in zip(own, top)]
     total = [jnp.sum(w, axis=1, keepdims=True) + o for w, o in zip(weights, own_weight)]
-    probs = [(w / t).astype(BF16) for w, t in zip(weights, total)]
-    own_prob = [(o / t).astype(BF16).astype(F32) for o, t in zip(own_weight, total)]
+    inverse = [1.0 / t for t in total]
+    probs = [(w * r).astype(BF16) for w, r in zip(weights, inverse)]
+    own_prob = [(o * r).astype(BF16).astype(F32) for o, r in zip(own_weight, inverse)]
     mixed = [jnp.dot(p, v, preferred_element_type=F32) for p, v in zip(probs, values)]
     return [
         (m + o * v.astype(F32)).astype(BF16) for m, o, v in zip(mixed, own_prob, own_values)

time: 27.1 us -> 27.1 us (level)
  no operation moved by 1% of the time
where the time goes in v7:
time: 27.1 us; the launch traced here: 27 us
  Pallas kernels  26.4 us (97%)
  between operations  0.64 us (2%)
    pallas_call x1, Pallas kernels, on_device(): pl.pallas_call(functools.partial(kernel, n_inst, n_tp), out_shape=out_sha...  25.7 us
    pallas_call x1, Pallas kernels, on_device(): pl.pallas_call(hand_over, out_shape=out_shape, in_specs=[pl.BlockSpec(mem...  0.65 us

profile of v7, /device:TPU:1, one launch (start us, length us, event | category | flops | bytes accessed | tf_op | source)
XLA Modules:
  0.0 27.0 jit_solution(13927249968617866635)
XLA Ops:
  0.6 25.7 %shard_map.131 = (bf16[8,4096]{1,0:T(8,128)(2,1)S(1)}, bf16[1,4096]{1,0:T(2,128)(2,1)S(1)}) custom-call(bf16[8,1024]{1,0:T(8,128)(2,1)} %queries.1, bf16[8,512,128]{2,1,0:T(8,128)(2,1)} %key_cache.1, bf16[8,512,128]{2,1,0:T(8,128)(2,1)} %value_cache.1, bf16[8,128]{1,0:T(8,128)(2,1)} %fresh_keys.1, bf16[8,128]{1,0:T(8,128)(2,1)} %fresh_values.1, ...), custom_call_target="tpu_custom_call" | custom-call | tf_op jit(solution)/shard_map/pallas_call | solution.py:284
  26.4 0.7 %shard_map.132 = (bf16[8,4096]{1,0:T(8,128)(2,1)}, bf16[1,4096]{1,0:T(2,128)(2,1)}) custom-call(bf16[8,4096]{1,0:T(8,128)(2,1)S(1)} %get-tuple-element.4.resident, bf16[1,4096]{1,0:T(2,128)(2,1)S(1)} %get-tuple-element.5.migrant), custom_call_target="tpu_custom_call" | custom-call | tf_op jit(solution)/shard_map/pallas_call | solution.py:323
